TPU v7x, 32 devices: a whole 2x2x4 slice. The times are simulated.
32 devices in a mesh: groups: 2 (over x), node: 2 (over core), local: 8 (over z, y).
Axes of the slice: x: 2, y: 2, z: 4, core: 2. Of those that a mesh axis runs over, the one named last changes fastest.
Arguments:
- tokens: bfloat16 [512, 7168], P(('groups', 'node', 'local')), parts along dimension 0, may hold values from -6 to 6
- expert_ids: int32 [512, 4], P(('groups', 'node', 'local')), parts along dimension 0, may hold values from 0 to 7, all different within a row; in each aligned block of 16 rows (0 to 15, 16 to 31, ...) at most 12 rows name the same one
- gate_weight: bfloat16 [512, 4], P(('groups', 'node', 'local')), parts along dimension 0, may hold values from 0.099609375 to 1
- expert_map: int32 [8], replicated, may hold values from 0 to 7, each once
- w_gate: bfloat16 [16, 7168, 512], P(('node', 'local')), may hold values from -0.0625 to 0.0625
- w_up: bfloat16 [16, 7168, 512], P(('node', 'local')), may hold values from -0.0625 to 0.0625
- w_down: bfloat16 [16, 512, 7168], P(('node', 'local')), may hold values from -0.1875 to 0.1875
Outputs:
- moe_out: bfloat16 [512, 7168], P(('groups', 'node', 'local')), parts along dimension 0
There are 2 independent parts, one for each index of `groups`. A program takes and returns all parts, laid end to end along the dimension named above; an argument that names none is the same for every part. Nothing has to cross between parts.
Inputs may be any that keep to these rules, and one draw needn't show every extreme that they name: `expert_ids`: each row names 4 different experts; among the rows of one device no expert is named by more than 12 rows, a bound that some block reaches. `expert_map`: each slot holds exactly one expert; slot s is shards 2 s and 2 s + 1, on the devices with those indices along node+local.
All inputs are finite; a program needn't handle non-finite values.
Results may differ from a plain program's by a relative error of at most 0.0085.
Values may be sent and summed in bfloat16 or wider, within the bound.
A program may use at most 128 MiB of HBM per device.

v0:
```python
import jax
import jax.numpy as jnp
from jax import lax
from jax.sharding import PartitionSpec as P


def expert_rows(routed_rows, routed_gates, w_gate, w_up, w_down):
    model_width = routed_rows.shape[-1]
    flat_rows = routed_rows.reshape(-1, model_width)
    gate_proj = jnp.dot(flat_rows, w_gate[0], preferred_element_type=jnp.float32)
    up_proj = jnp.dot(flat_rows, w_up[0], preferred_element_type=jnp.float32)
    hidden = (jax.nn.silu(gate_proj) * up_proj).astype(jnp.bfloat16)
    down_proj = jnp.dot(hidden, w_down[0], preferred_element_type=jnp.float32)
    scaled = down_proj * routed_gates.reshape(-1, 1).astype(jnp.float32)
    return scaled.astype(jnp.bfloat16).reshape(routed_rows.shape)


def slot_lookup(route_ids, expert_map):
    expert_count = expert_map.shape[0]
    matches = route_ids[:, :, None] == jnp.arange(expert_count, dtype=jnp.int32)[None, None, :]
    return jnp.sum(jnp.where(matches, expert_map[None, None, :], 0), axis=2)


def select_tables(slot_ids, route_gates, first_slot, slot_count, capacity):
    wanted = first_slot + jnp.arange(slot_count, dtype=jnp.int32)
    matches = slot_ids[None, :, :] == wanted[:, None, None]
    member = jnp.any(matches, axis=2)
    weights = jnp.sum(jnp.where(matches, route_gates[None, :, :].astype(jnp.float32), 0.0), axis=2)
    position = jnp.cumsum(member.astype(jnp.int32), axis=1) - 1
    places = jnp.arange(capacity, dtype=jnp.int32)[None, :, None]
    picked = member[:, None, :] & (position[:, None, :] == places)
    picker = picked.astype(jnp.bfloat16)
    slot_gates = jnp.einsum("jct,jt->jc", picked.astype(jnp.float32), weights).astype(jnp.bfloat16)
    return (picker, slot_gates)


def pack_rows(picker, source_rows):
    packed = jnp.einsum("jct,td->jcd", picker, source_rows, preferred_element_type=jnp.float32)
    return packed.astype(jnp.bfloat16)


def unpack_sums(picker, returned):
    slot_count, capacity, _ = picker.shape
    halves = returned.reshape(slot_count, 2, capacity, returned.shape[-1])
    return jnp.einsum("jct,jhcd->td", picker, halves, preferred_element_type=jnp.float32)


def body(tokens, expert_ids, gate_weight, expert_map, w_gate, w_up, w_down):
    tok_count = tokens.shape[0]
    top_count = expert_ids.shape[1]
    expert_count = expert_map.shape[0]
    most_rows = 3 * tok_count * top_count // (2 * expert_count)
    node_count = lax.axis_size("node")
    per_node = lax.axis_size("local") // 2
    capacity = node_count * most_rows
    all_rows, all_ids, all_gates = (
        lax.all_gather(tokens, "node", axis=0, tiled=True),
        lax.all_gather(expert_ids, "node", axis=0, tiled=True),
        lax.all_gather(gate_weight, "node", axis=0, tiled=True),
    )
    slot_ids = slot_lookup(all_ids, expert_map)
    first_slot = lax.axis_index("node") * per_node
    picker, slot_gates = select_tables(slot_ids, all_gates, first_slot, per_node, capacity)
    send_rows = jnp.repeat(pack_rows(picker, all_rows), 2, axis=0)
    send_gates = jnp.repeat(slot_gates, 2, axis=0)
    part_rows = expert_rows(
        lax.all_to_all(send_rows, "local", split_axis=0, concat_axis=0, tiled=True),
        lax.all_to_all(send_gates, "local", split_axis=0, concat_axis=0, tiled=True),
        w_gate,
        w_up,
        w_down,
    )
    returned = lax.all_to_all(part_rows, "local", split_axis=0, concat_axis=0, tiled=True)
    node_total = unpack_sums(picker, returned)
    total = lax.psum_scatter(node_total, "node", scatter_dimension=0, tiled=True)
    return total.astype(jnp.bfloat16)


def solution(mesh):
    return jax.shard_map(
        body,
        mesh=mesh,
        in_specs=(
            P(("groups", "node", "local"), None),
            P(("groups", "node", "local"), None),
            P(("groups", "node", "local"), None),
            P(),
            P(("node", "local"), None, None),
            P(("node", "local"), None, None),
            P(("node", "local"), None, None),
        ),
        out_specs=P(("groups", "node", "local"), None),
        check_vma=False,
    )
```

profile of v0, /device:TPU:0, one launch (start us, length us, event | category | flops | bytes accessed | tf_op | source)
XLA Modules:
  0.0 191.8 jit_solution(2022174265990129398)
XLA Ops:
  6.5 2.1 %all-gather.1 = bf16[2,16,4]{1,2,0:T(4,128)(2,1)S(1)} all-gather(bf16[1,16,4]{1,2,0:T(4,128)(2,1)} %bitcast.49), channel_id=1, replica_groups=mesh['groups'=2,'node'=2,'local'=8] {'node'}, dimensions={0}, use_global_device_ids=true | all-gather | bytes 384 | tf_op jit(solution)/shard_map/all_gather | solution.py:59
  8.7 0.1 reshape.55
  8.7 1.9 %all-gather = s32[2,16,4]{1,2,0:T(4,128)S(1)} all-gather(s32[1,16,4]{1,2,0:T(4,128)} %bitcast.46), channel_id=1, replica_groups=mesh['groups'=2,'node'=2,'local'=8] {'node'}, dimensions={0}, use_global_device_ids=true | all-gather | bytes 768 | tf_op jit(solution)/shard_map/all_gather | solution.py:58
  10.7 0.1 reshape.52
  10.8 0.7 select_reduce_fusion
  11.5 0.1 compare_reduce_fusion
  11.6 0.1 fusion.32
  11.7 0.2 reduce_window_sum.11
  11.9 0.1 fusion.23
  12.0 0.6 copy.23
  12.6 7.1 %all-to-all-start.1 = ((bf16[8,1,24]{2,1,0:T(2,128)(2,1)}), bf16[8,1,24]{2,1,0:T(2,128)(2,1)S(1)}, u32[]{:S(2)}, u32[]{:S(2)}) async-start(bf16[8,1,24]{2,1,0:T(2,128)(2,1)} %copy.23), calls=%async_computation.1 | async-start | bytes 8192 | tf_op jit(solution)/shard_map/all_to_all | solution.py:68
  19.8 2.3 %all_gather.10 = bf16[32,7168]{1,0:T(8,128)(2,1)S(1)} all-gather(bf16[16,7168]{1,0:T(8,128)(2,1)} %param.7), channel_id=1, replica_groups=mesh['groups'=2,'node'=2,'local'=8] {'node'}, dimensions={0}, use_global_device_ids=true | all-gather | bytes 688128 | tf_op jit(solution)/shard_map/all_gather | solution.py:57
  22.1 0.5 convolution_convert_fusion
  22.6 3.6 %all-to-all-done.1 = bf16[8,1,24]{2,1,0:T(2,128)(2,1)S(1)} async-done(((bf16[8,1,24]{2,1,0:T(2,128)(2,1)}), bf16[8,1,24]{2,1,0:T(2,128)(2,1)S(1)}, u32[]{:S(2)}, u32[]{:S(2)}) %all-to-all-start.1) | async-done | bytes 416 | tf_op jit(solution)/shard_map/all_to_all | solution.py:68
  26.2 1.9 broadcast_in_dim.41
  28.0 3.6 %all-to-all-start = ((bf16[8,24,7168]{2,1,0:T(8,128)(2,1)}), bf16[8,24,7168]{2,1,0:T(8,128)(2,1)S(1)}, u32[]{:S(2)}, u32[]{:S(2)}) async-start(bf16[8,24,7168]{2,1,0:T(8,128)(2,1)} %bitcast.2), calls=%async_computation | async-start | bytes 5505024 | tf_op jit(solution)/shard_map/all_to_all | solution.py:67
  31.7 0.0 reduce-scatter.2.cloned.1.call-start
  31.8 0.1 reshape.49
  31.8 61.3 %all-to-all-done = bf16[8,24,7168]{2,1,0:T(8,128)(2,1)S(1)} async-done(((bf16[8,24,7168]{2,1,0:T(8,128)(2,1)}), bf16[8,24,7168]{2,1,0:T(8,128)(2,1)S(1)}, u32[]{:S(2)}, u32[]{:S(2)}) %all-to-all-start) | async-done | bytes 2752544 | tf_op jit(solution)/shard_map/all_to_all | solution.py:67
  93.1 4.7 %fusion.4 = f32[192,512]{1,0:T(8,128)S(1)} fusion(bf16[192,7168]{1,0:T(8,128)(2,1)S(1)} %bitcast.42, bf16[1,7168,512]{2,1,0:T(8,128)(2,1)} %param.11), kind=kOutput, calls=%fused_computation.7 | convolution fusion | flops 1409286144 | bytes 10485760 | tf_op jit(solution)/shard_map/dot_general | solution.py:10
  97.8 10.0 %fusion = bf16[192,7168]{1,0:T(8,128)(2,1)} fusion(bf16[1,512,7168]{2,1,0:T(8,128)(2,1)} %param.13, f32[192]{0:T(256)S(1)} %reshape.49, bf16[192,7168]{1,0:T(8,128)(2,1)S(1)} %bitcast.43, bf16[1,7168,512]{2,1,0:T(8,128)(2,1)} %param.12, f32[192,512]{1,0:T(8,128)S(1)} %fusion.4), kind=kOutput, calls=%fused_computation.1 | convolution fusion | flops 2821914624 | bytes 20579072 | tf_op jit(solution)/shard_map/dot_general | solution.py:13
  107.8 66.4 %all_to_all.19 = bf16[8,24,7168]{2,1,0:T(8,128)(2,1)S(1)} all-to-all(bf16[8,24,7168]{2,1,0:T(8,128)(2,1)} %bitcast.44), channel_id=1, replica_groups=mesh['groups'=2,'node'=2,'local'=8] {'local'}, dimensions={0} | all-to-all | bytes 5505024 | tf_op jit(solution)/shard_map/all_to_all | solution.py:73
  174.2 0.5 convert_reduce_fusion
  174.7 1.3 convolution_bitcast_fusion
  176.0 0.0 reduce-scatter.2.cloned.1.call-update
  176.0 7.3 %reduce-scatter.2.cloned.1.call-done = f32[16,7168]{1,0:T(8,128)} async-done(((f32[32,7168]{1,0:T(8,128)}), f32[16,7168]{1,0:T(8,128)}) %reduce-scatter.2.cloned.1.call-update) | async-done | bytes 458768 | tf_op jit(solution)/shard_map/reduce_scatter | solution.py:75
  183.2 1.7 convert_element_type.55
  (8 shorter events, 0.0 us)
Async XLA Ops:
  12.6 13.5 %all-to-all-start.1 = ((bf16[8,1,24]{2,1,0:T(2,128)(2,1)}), bf16[8,1,24]{2,1,0:T(2,128)(2,1)S(1)}, u32[]{:S(2)}, u32[]{:S(2)}) async-start(bf16[8,1,24]{2,1,0:T(2,128)(2,1)} %copy.23), calls=%async_computation.1 | async-start | bytes 8192 | tf_op jit(solution)/shard_map/all_to_all | solution.py:68
  28.0 65.1 %all-to-all-start = ((bf16[8,24,7168]{2,1,0:T(8,128)(2,1)}), bf16[8,24,7168]{2,1,0:T(8,128)(2,1)S(1)}, u32[]{:S(2)}, u32[]{:S(2)}) async-start(bf16[8,24,7168]{2,1,0:T(8,128)(2,1)} %bitcast.2), calls=%async_computation | async-start | bytes 5505024 | tf_op jit(solution)/shard_map/all_to_all | solution.py:67
  31.7 151.6 %reduce-scatter.2.cloned.1.call-start = ((), (), s32[]{:S(2)}) async-start(), calls=%async_computation.4 | async-start | bytes 1376256 | tf_op jit(solution)/shard_map/reduce_scatter | solution.py:75
Sparse Core Ops, SparseCore 0:
  176.1 7.0 reduce-scatter.1
where the time goes:
time: 192 us
  blocking collectives  72.8 us (38%)
  waiting for transfers between devices  72.1 us (38%)
  matrix products  16.6 us (9%)
  between operations  13.4 us (7%)
  starting transfers between devices  10.8 us (6%)
  other arithmetic  3.35 us (2%)
  local copies, waits for them, and re-layouts  2.73 us (1%)
    all_to_all x1, blocking collectives, body(): lax.all_to_all(part_rows, 'local', split_axis=0, concat_axis=0, tiled=True)  66.4 us
    all_to_all x1, waiting for transfers between devices, body(): lax.all_to_all(send_rows, 'local', split_axis=0, concat_axis=0, tiled=True)  61.3 us
    dot_general x1, matrix products, expert_rows(): down_proj = jnp.dot(hidden, w_down[0], preferred_element_type=jnp.float32)  9.97 us
    reduce_scatter x1, waiting for transfers between devices, body(): lax.psum_scatter(node_total, 'node', scatter_dimension=0, tiled=True)  7.25 us
    all_to_all x1, starting transfers between devices, body(): lax.all_to_all(send_gates, 'local', split_axis=0, concat_axis=0, tiled=True)  7.13 us
    dot_general x1, matrix products, expert_rows(): jnp.dot(flat_rows, w_gate[0], preferred_element_type=jnp.float32)  4.71 us
  transfers between devices with their start and end apart: 3, of which 3 were waited for; matrix products, arithmetic and copies ran while one was open for 0% of the time, Pallas kernels for 0%

commit v1 on v0

v1 whole, which is shorter than its diff:
```python
import functools

import jax
import jax.numpy as jnp
from jax import lax
from jax.experimental import pallas as pl
from jax.experimental.pallas import tpu as pltpu
from jax.sharding import PartitionSpec as P

LANES = 128
GROUP = 2
PARTS_W = 4


def ring_kernel(
    n, ids_ref, gates_ref, map_ref, tokens_ref, wg_hbm, wu_hbm, wd_hbm, out_ref,
    xg, part, insib, rsin, wg, wu, wd,
    tok_sem, w_sem, ag_send, ag_recv, sx_send, sx_recv, sp_send, sp_recv, rs_send, rs_recv,
):
    rows, width = out_ref.shape
    hid = wg.shape[1]
    half = width // LANES // 2 * LANES
    x_cols = ((0, half), (half, width + LANES - half))
    y_cols = ((0, half), (half, width - half))
    pieces = len(x_cols)

    node = lax.axis_index("node")
    local = lax.axis_index("local")
    row_z, row_y = local // 2, local % 2
    pos = row_z * (1 - row_y) + (n - 1 - row_z) * row_y
    step = 1 - 2 * node

    def at(place):
        place = (place + n) % n
        late = place // (n // 2)
        return 2 * place * (1 - late) + (2 * (n - 1 - place) + 1) * late

    ahead = {"local": at(pos + step)}
    behind = {"local": at(pos - step)}
    sibling = {"node": 1 - node}

    tok_copy = pltpu.make_async_copy(tokens_ref, xg.at[pl.ds(0, rows), pl.ds(0, width)], tok_sem)
    tok_copy.start()
    w_copies = []
    for m, (src, dst) in enumerate(((wg_hbm, wg), (wu_hbm, wu), (wd_hbm, wd))):
        span = dst.shape[0] // PARTS_W
        copies = []
        for q in range(PARTS_W):
            block = pl.ds(q * span, span)
            copies.append(pltpu.make_async_copy(src.at[0, block], dst.at[block], w_sem.at[m, q]))
        w_copies.append(copies)
    for q in range(PARTS_W):
        w_copies[0][q].start()
        w_copies[1][q].start()
    for q in range(PARTS_W):
        w_copies[2][q].start()

    lane = lax.broadcasted_iota(jnp.int32, (rows, LANES), 1)
    weights = jnp.zeros((rows, LANES), jnp.float32)
    for k in range(ids_ref.shape[1]):
        weights += jnp.where(ids_ref[:, k:k + 1] == lane, gates_ref[:, k:k + 1].astype(jnp.float32), 0.0)
    xg[0:rows, width:width + LANES] = weights.astype(xg.dtype)

    lane_row = lax.broadcasted_iota(jnp.int32, (1, LANES), 1)
    slots = jnp.full((1, LANES), -1, jnp.int32)
    for e in range(map_ref.shape[0]):
        slots = jnp.where(lane_row == e, map_ref[e], slots)
    chosen = (slots == (node * n + local) // 2).astype(jnp.float32)

    barrier = pltpu.get_barrier_semaphore()
    for device in (ahead, behind, sibling):
        pl.semaphore_signal(barrier, inc=1, device_id=device, device_id_type=pl.DeviceIdType.MESH)
    pl.semaphore_wait(barrier, 3)
    tok_copy.wait()

    def remote(src, dst, send, recv, device):
        return pltpu.make_async_remote_copy(
            src_ref=src, dst_ref=dst, send_sem=send, recv_sem=recv,
            device_id=device, device_id_type=pl.DeviceIdType.MESH,
        )

    def x_block(s, who, h):
        return xg.at[pl.ds((2 * s + who) * rows, rows), pl.ds(*x_cols[h])]

    def gather_copy(s, h):
        return remote(x_block(s - 1, 0, h), x_block(s, 0, h), ag_send.at[s, h], ag_recv.at[s, h], ahead)

    def mirror_copy(s, h):
        return remote(x_block(s, 0, h), x_block(s, 1, h), sx_send.at[s, h], sx_recv.at[s, h], sibling)

    def give_copy(s, h):
        cols = pl.ds(*y_cols[h])
        return remote(
            part.at[pl.ds((2 * s + 1) * rows, rows), cols], insib.at[pl.ds(s * rows, rows), cols],
            sp_send.at[s, h], sp_recv.at[s, h], sibling,
        )

    def sum_copy(s, h):
        cols = pl.ds(*y_cols[h])
        return remote(
            part.at[pl.ds(2 * s * rows, rows), cols], rsin.at[pl.ds(s * rows, rows), cols],
            rs_send.at[s, h], rs_recv.at[s, h], ahead,
        )

    def gather(s):
        for h in range(pieces):
            if s > 0:
                gather_copy(s, h).wait_recv()
            if s < n - 1:
                gather_copy(s + 1, h).start()
            mirror_copy(s, h).start()

    group_rows = GROUP * 2 * rows
    k_tile = width // 4
    n_tile = width // 14

    def hidden_of(g):
        for s in range(g * GROUP, g * GROUP + GROUP):
            for h in range(pieces):
                mirror_copy(s, h).wait_recv()
        if g == 0:
            for copy in w_copies[0] + w_copies[1]:
                copy.wait()
        first = g * group_rows

        def add(k, sums):
            span = pl.ds(pl.multiple_of(k * k_tile, k_tile), k_tile)
            x = xg[pl.ds(first, group_rows), span]
            return (
                sums[0] + jnp.dot(x, wg[span, :], preferred_element_type=jnp.float32),
                sums[1] + jnp.dot(x, wu[span, :], preferred_element_type=jnp.float32),
            )

        zero = jnp.zeros((group_rows, hid), jnp.float32)
        gate, up = lax.fori_loop(0, width // k_tile, add, (zero, zero))
        return (gate / (1.0 + jnp.exp(-gate)) * up).astype(jnp.bfloat16)

    def down(g, hidden):
        if g == 0:
            for copy in w_copies[2]:
                copy.wait()
        first = g * group_rows
        coef = jnp.sum(
            xg[pl.ds(first, group_rows), pl.ds(width, LANES)].astype(jnp.float32) * chosen, axis=1, keepdims=True
        )

        def tile(j, carry):
            span = pl.ds(pl.multiple_of(j * n_tile, n_tile), n_tile)
            y = jnp.dot(hidden, wd[:, span], preferred_element_type=jnp.float32)
            part[pl.ds(first, group_rows), span] = (y * coef).astype(part.dtype)
            return carry

        for h in range(pieces):
            lax.fori_loop(h * 14 // pieces, (h + 1) * 14 // pieces, tile, 0)
            for s in range(g * GROUP, g * GROUP + GROUP):
                give_copy(s, h).start()

    def total(s, h):
        cols = pl.ds(*y_cols[h])
        give_copy(s, h).wait_recv()
        value = part[pl.ds(2 * s * rows, rows), cols].astype(jnp.float32)
        value += insib[pl.ds(s * rows, rows), cols].astype(jnp.float32)
        before = n - 1 if s == 0 else s - 1
        if before > 0:
            sum_copy(before, h).wait_recv()
            value += rsin[pl.ds(before * rows, rows), cols].astype(jnp.float32)
        return value

    def reduce(s):
        for h in range(pieces):
            part[pl.ds(2 * s * rows, rows), pl.ds(*y_cols[h])] = total(s, h).astype(part.dtype)
            sum_copy(s, h).start()

    groups = n // GROUP
    for s in range(3):
        gather(s)
    for g in range(groups):
        hidden = hidden_of(g)
        if g > 0:
            for s in range((g - 1) * GROUP, g * GROUP):
                if s > 0:
                    reduce(s)
        if 2 * g + 3 < n:
            gather(2 * g + 3)
        down(g, hidden)
        if 2 * g + 4 < n:
            gather(2 * g + 4)
    for s in range((groups - 1) * GROUP, n):
        reduce(s)
    for h in range(pieces):
        out_ref[:, y_cols[h][0]:y_cols[h][0] + y_cols[h][1]] = total(0, h).astype(out_ref.dtype)

    for s in range(n):
        for h in range(pieces):
            mirror_copy(s, h).wait_send()
            give_copy(s, h).wait_send()
            if s > 0:
                gather_copy(s, h).wait_send()
                sum_copy(s, h).wait_send()


def body(n, tokens, expert_ids, gate_weight, expert_map, w_gate, w_up, w_down):
    rows, width = tokens.shape
    hid = w_gate.shape[2]
    any_spec = pl.BlockSpec(memory_space=pl.ANY)
    vmem_spec = pl.BlockSpec(memory_space=pltpu.VMEM)
    dma = pltpu.SemaphoreType.DMA
    bf16 = jnp.bfloat16
    flops = 2 * 2 * n * rows * width * hid * 3
    moved = 3 * width * hid * 2
    return pl.pallas_call(
        functools.partial(ring_kernel, n),
        out_shape=jax.ShapeDtypeStruct((rows, width), bf16),
        in_specs=[vmem_spec, vmem_spec, pl.BlockSpec(memory_space=pltpu.SMEM)] + [any_spec] * 4,
        out_specs=vmem_spec,
        scratch_shapes=[
            pltpu.VMEM((2 * n * rows, width + LANES), bf16),
            pltpu.VMEM((2 * n * rows, width), bf16),
            pltpu.VMEM((n * rows, width), bf16),
            pltpu.VMEM((n * rows, width), bf16),
            pltpu.VMEM((width, hid), bf16),
            pltpu.VMEM((width, hid), bf16),
            pltpu.VMEM((hid, width), bf16),
            dma,
            dma((3, PARTS_W)),
        ] + [dma((n, 2))] * 8,
        compiler_params=pltpu.CompilerParams(
            collective_id=0, has_side_effects=True, vmem_limit_bytes=58 * 1024 * 1024
        ),
        cost_estimate=pl.CostEstimate(flops=flops, bytes_accessed=moved, transcendentals=2 * n * rows * hid),
    )(expert_ids, gate_weight, expert_map, tokens, w_gate, w_up, w_down)


def solution(mesh):
    return jax.shard_map(
        functools.partial(body, mesh.shape["local"]),
        mesh=mesh,
        in_specs=(
            P(("groups", "node", "local"), None),
            P(("groups", "node", "local"), None),
            P(("groups", "node", "local"), None),
            P(),
            P(("node", "local"), None, None),
            P(("node", "local"), None, None),
            P(("node", "local"), None, None),
        ),
        out_specs=P(("groups", "node", "local"), None),
        check_vma=False,
    )
```

time: 192 us -> 74.4 us (0.39)
  blocking collectives: 72.8 us -> 0 us
  waiting for transfers between devices: 72.1 us -> 0 us
  Pallas kernels: 0 us -> 69.7 us
  matrix products: 16.6 us -> 0 us
  between operations: 13.4 us -> 0.01 us
  starting transfers between devices: 10.8 us -> 0 us
  other arithmetic: 3.35 us -> 0 us
    pallas_call x0 -> x1, Pallas kernels: none -> 69.7 us  [body(): pl.pallas_call(functools.partial(ring_kernel, n), out_shape=jax.ShapeDtyp...]
    all_to_all x1 -> x0, blocking collectives: 66.4 us -> none  [body(): lax.all_to_all(part_rows, 'local', split_axis=0, concat_axis=0, tiled=True)]
    all_to_all x2 -> x0, waiting for transfers between devices: 64.8 us -> none  [the longest x1 61.3 us: body(): lax.all_to_all(send_rows, 'local', split_axis=0, concat_axis=0, tiled=True)]
    dot_general x5 -> x0, matrix products: 16.6 us -> none  [the longest x1 9.97 us: expert_rows(): down_proj = jnp.dot(hidden, w_down[0], preferred_element_type=jnp.float32)]
    all_to_all x2 -> x0, starting transfers between devices: 10.8 us -> none  [the longest x1 7.13 us: body(): lax.all_to_all(send_gates, 'local', split_axis=0, concat_axis=0, tiled=True)]
    reduce_scatter x1 -> x0, waiting for transfers between devices: 7.25 us -> none  [body(): lax.psum_scatter(node_total, 'node', scatter_dimension=0, tiled=True)]
    all_gather x3 -> x0, blocking collectives: 6.37 us -> none  [the longest x1 2.33 us: body(): lax.all_gather(tokens, 'node', axis=0, tiled=True)]
    unnamed x1 -> x3, local copies, waits for them, and re-layouts: 0.08 us -> 4.34 us
  transfers between devices with their start and end apart: 3 -> 0, of which waited for: 3 -> 0; matrix products, arithmetic and copies ran while one was open for 0% -> 0% of each run, Pallas kernels for 0% -> 0%
where the time goes in v1:
time: 74.4 us; the launch traced here: 74 us
  Pallas kernels  69.7 us (94%)
  local copies, waits for them, and re-layouts  4.34 us (6%)
    pallas_call x1, Pallas kernels, body(): pl.pallas_call(functools.partial(ring_kernel, n), out_shape=jax.ShapeDtyp...  69.7 us
    unnamed x3, local copies, waits for them, and re-layouts  4.34 us

profile of v1, /device:TPU:0, one launch (start us, length us, event | category | flops | bytes accessed | tf_op | source)
XLA Modules:
  0.0 74.0 jit_solution(15299395970454400687)
XLA Ops:
  0.0 1.3 %copy.9.gates_ref = bf16[16,4]{1,0:T(8,128)(2,1)} copy(bf16[16,4]{0,1:T(4,128)(2,1)} %param.9) | data formatting | bytes 256 | tf_op args[2]
  1.3 1.4 %copy.8.ids_ref = s32[16,4]{1,0:T(8,128)} copy(s32[16,4]{0,1:T(4,128)} %param.8) | data formatting | bytes 512 | tf_op args[1]
  2.7 69.7 %shard_map.73 = bf16[16,7168]{1,0:T(8,128)(2,1)} custom-call(s32[16,4]{1,0:T(8,128)} %copy.8.ids_ref, bf16[16,4]{1,0:T(8,128)(2,1)} %copy.9.gates_ref, s32[8]{0:T(128)} %map_ref.1, bf16[16,7168]{1,0:T(8,128)(2,1)} %tokens_ref.1, bf16[1,7168,512]{2,1,0:T(8,128)(2,1)} %wg_hbm.1, bf16[1,7168,512]{2,1,0:T(8,128)(2,1)} %wu_hbm.1, bf16[1,512,7168]{2,1,0:T(8,128)(2,1)} %wd_hbm.1), custom_call_target="tpu_custom_call" | custom-call | flops 5637144576 | bytes 22020096 | tf_op jit(solution)/shard_map/pallas_call | solution.py:211
  72.4 1.6 %copy.11 = bf16[16,7168]{1,0:T(8,128)(2,1)} copy(bf16[16,7168]{1,0:T(8,128)(2,1)} %shard_map.73) | data formatting | bytes 458752

commit v2 on v1

--- a/solution.py
+++ b/solution.py
@@ -9,6 +9,7 @@
 
 LANES = 128
 GROUP = 2
+PIECES = 4
 PARTS_W = 4
 
 
@@ -19,10 +20,10 @@
 ):
     rows, width = out_ref.shape
     hid = wg.shape[1]
-    half = width // LANES // 2 * LANES
-    x_cols = ((0, half), (half, width + LANES - half))
-    y_cols = ((0, half), (half, width - half))
-    pieces = len(x_cols)
+    pieces = PIECES
+    span_w = width // pieces
+    y_cols = [(h * span_w, span_w) for h in range(pieces)]
+    x_cols = y_cols[:-1] + [(width - span_w, span_w + LANES)]
 
     node = lax.axis_index("node")
     local = lax.axis_index("local")
@@ -39,7 +40,7 @@
     behind = {"local": at(pos - step)}
     sibling = {"node": 1 - node}
 
-    tok_copy = pltpu.make_async_copy(tokens_ref, xg.at[pl.ds(0, rows), pl.ds(0, width)], tok_sem)
+    tok_copy = pltpu.make_async_copy(tokens_ref, xg.at[pl.ds((2 * n - 2) * rows, rows), pl.ds(0, width)], tok_sem)
     tok_copy.start()
     w_copies = []
     for m, (src, dst) in enumerate(((wg_hbm, wg), (wu_hbm, wu), (wd_hbm, wd))):
@@ -55,11 +56,16 @@
     for q in range(PARTS_W):
         w_copies[2][q].start()
 
-    lane = lax.broadcasted_iota(jnp.int32, (rows, LANES), 1)
-    weights = jnp.zeros((rows, LANES), jnp.float32)
-    for k in range(ids_ref.shape[1]):
-        weights += jnp.where(ids_ref[:, k:k + 1] == lane, gates_ref[:, k:k + 1].astype(jnp.float32), 0.0)
-    xg[0:rows, width:width + LANES] = weights.astype(xg.dtype)
+    expert = lax.broadcasted_iota(jnp.int32, (LANES, rows), 0)
+    weights = jnp.zeros((LANES, rows), jnp.float32)
+    for k in range(ids_ref.shape[0]):
+        weights += jnp.where(ids_ref[k:k + 1, :] == expert, gates_ref[k:k + 1, :].astype(jnp.float32), 0.0)
+    same = lax.broadcasted_iota(jnp.int32, (rows, rows), 0) == lax.broadcasted_iota(jnp.int32, (rows, rows), 1)
+    weights = lax.dot_general(
+        same.astype(jnp.float32).astype(jnp.bfloat16), weights.astype(jnp.bfloat16), (((1,), (1,)), ((), ())),
+        preferred_element_type=jnp.float32,
+    )
+    xg[(2 * n - 2) * rows:(2 * n - 1) * rows, width:width + LANES] = weights.astype(xg.dtype)
 
     lane_row = lax.broadcasted_iota(jnp.int32, (1, LANES), 1)
     slots = jnp.full((1, LANES), -1, jnp.int32)
@@ -79,8 +85,11 @@
             device_id=device, device_id_type=pl.DeviceIdType.MESH,
         )
 
+    def slot(s, who):
+        return pl.ds((2 * ((s - 1) % n) + who) * rows, rows)
+
     def x_block(s, who, h):
-        return xg.at[pl.ds((2 * s + who) * rows, rows), pl.ds(*x_cols[h])]
+        return xg.at[slot(s, who), pl.ds(*x_cols[h])]
 
     def gather_copy(s, h):
         return remote(x_block(s - 1, 0, h), x_block(s, 0, h), ag_send.at[s, h], ag_recv.at[s, h], ahead)
@@ -91,51 +100,50 @@
     def give_copy(s, h):
         cols = pl.ds(*y_cols[h])
         return remote(
-            part.at[pl.ds((2 * s + 1) * rows, rows), cols], insib.at[pl.ds(s * rows, rows), cols],
+            part.at[slot(s, 1), cols], insib.at[pl.ds(s * rows, rows), cols],
             sp_send.at[s, h], sp_recv.at[s, h], sibling,
         )
 
     def sum_copy(s, h):
         cols = pl.ds(*y_cols[h])
         return remote(
-            part.at[pl.ds(2 * s * rows, rows), cols], rsin.at[pl.ds(s * rows, rows), cols],
+            part.at[slot(s, 0), cols], rsin.at[pl.ds(s * rows, rows), cols],
             rs_send.at[s, h], rs_recv.at[s, h], ahead,
         )
 
-    def gather(s):
-        for h in range(pieces):
-            if s > 0:
-                gather_copy(s, h).wait_recv()
-            if s < n - 1:
-                gather_copy(s + 1, h).start()
-            mirror_copy(s, h).start()
+    def gather(s, h):
+        if s > 0:
+            gather_copy(s, h).wait_recv()
+        if s < n - 1:
+            gather_copy(s + 1, h).start()
+        mirror_copy(s, h).start()
 
     group_rows = GROUP * 2 * rows
-    k_tile = width // 4
-    n_tile = width // 14
-
-    def hidden_of(g):
-        for s in range(g * GROUP, g * GROUP + GROUP):
+    k_tile = width // PIECES
+    n_tile = width // PIECES
+
+    def chunks_of(g):
+        return [s % n for s in range(g * GROUP + 1, g * GROUP + GROUP + 1)]
+
+    def hidden_of(g, between):
+        for s in chunks_of(g):
             for h in range(pieces):
                 mirror_copy(s, h).wait_recv()
-        if g == 0:
-            for copy in w_copies[0] + w_copies[1]:
-                copy.wait()
         first = g * group_rows
-
-        def add(k, sums):
-            span = pl.ds(pl.multiple_of(k * k_tile, k_tile), k_tile)
+        gate = jnp.zeros((group_rows, hid), jnp.float32)
+        up = jnp.zeros((group_rows, hid), jnp.float32)
+        for k in range(pieces):
+            if g == 0:
+                w_copies[0][k].wait()
+                w_copies[1][k].wait()
+            span = pl.ds(k * k_tile, k_tile)
             x = xg[pl.ds(first, group_rows), span]
-            return (
-                sums[0] + jnp.dot(x, wg[span, :], preferred_element_type=jnp.float32),
-                sums[1] + jnp.dot(x, wu[span, :], preferred_element_type=jnp.float32),
-            )
-
-        zero = jnp.zeros((group_rows, hid), jnp.float32)
-        gate, up = lax.fori_loop(0, width // k_tile, add, (zero, zero))
+            gate += jnp.dot(x, wg[span, :], preferred_element_type=jnp.float32)
+            up += jnp.dot(x, wu[span, :], preferred_element_type=jnp.float32)
+            between(k)
         return (gate / (1.0 + jnp.exp(-gate)) * up).astype(jnp.bfloat16)
 
-    def down(g, hidden):
+    def down(g, hidden, between):
         if g == 0:
             for copy in w_copies[2]:
                 copy.wait()
@@ -143,22 +151,18 @@
         coef = jnp.sum(
             xg[pl.ds(first, group_rows), pl.ds(width, LANES)].astype(jnp.float32) * chosen, axis=1, keepdims=True
         )
-
-        def tile(j, carry):
-            span = pl.ds(pl.multiple_of(j * n_tile, n_tile), n_tile)
+        for h in range(pieces):
+            span = pl.ds(h * n_tile, n_tile)
             y = jnp.dot(hidden, wd[:, span], preferred_element_type=jnp.float32)
             part[pl.ds(first, group_rows), span] = (y * coef).astype(part.dtype)
-            return carry
-
-        for h in range(pieces):
-            lax.fori_loop(h * 14 // pieces, (h + 1) * 14 // pieces, tile, 0)
-            for s in range(g * GROUP, g * GROUP + GROUP):
+            for s in chunks_of(g):
                 give_copy(s, h).start()
+            between(h)
 
     def total(s, h):
         cols = pl.ds(*y_cols[h])
         give_copy(s, h).wait_recv()
-        value = part[pl.ds(2 * s * rows, rows), cols].astype(jnp.float32)
+        value = part[slot(s, 0), cols].astype(jnp.float32)
         value += insib[pl.ds(s * rows, rows), cols].astype(jnp.float32)
         before = n - 1 if s == 0 else s - 1
         if before > 0:
@@ -166,27 +170,30 @@
             value += rsin[pl.ds(before * rows, rows), cols].astype(jnp.float32)
         return value
 
-    def reduce(s):
+    def reduce(s, h):
+        part[slot(s, 0), pl.ds(*y_cols[h])] = total(s, h).astype(part.dtype)
+        sum_copy(s, h).start()
+
+    for h in range(pieces):
+        gather(0, h)
+    for s in (1, 2):
         for h in range(pieces):
-            part[pl.ds(2 * s * rows, rows), pl.ds(*y_cols[h])] = total(s, h).astype(part.dtype)
-            sum_copy(s, h).start()
+            gather(s, h)
+
+    def between(gather_step, reduce_step):
+        def run(h):
+            if gather_step < n:
+                gather(gather_step, h)
+            if 0 < reduce_step < n:
+                reduce(reduce_step, h)
+        return run
 
     groups = n // GROUP
-    for s in range(3):
-        gather(s)
     for g in range(groups):
-        hidden = hidden_of(g)
-        if g > 0:
-            for s in range((g - 1) * GROUP, g * GROUP):
-                if s > 0:
-                    reduce(s)
-        if 2 * g + 3 < n:
-            gather(2 * g + 3)
-        down(g, hidden)
-        if 2 * g + 4 < n:
-            gather(2 * g + 4)
-    for s in range((groups - 1) * GROUP, n):
-        reduce(s)
+        hidden = hidden_of(g, between(2 * g + 3, 2 * g - 1))
+        down(g, hidden, between(2 * g + 4, 2 * g))
+    for h in range(pieces):
+        reduce(n - 1, h)
     for h in range(pieces):
         out_ref[:, y_cols[h][0]:y_cols[h][0] + y_cols[h][1]] = total(0, h).astype(out_ref.dtype)
 
@@ -223,12 +230,12 @@
             pltpu.VMEM((hid, width), bf16),
             dma,
             dma((3, PARTS_W)),
-        ] + [dma((n, 2))] * 8,
+        ] + [dma((n, PIECES))] * 8,
         compiler_params=pltpu.CompilerParams(
             collective_id=0, has_side_effects=True, vmem_limit_bytes=58 * 1024 * 1024
         ),
         cost_estimate=pl.CostEstimate(flops=flops, bytes_accessed=moved, transcendentals=2 * n * rows * hid),
-    )(expert_ids, gate_weight, expert_map, tokens, w_gate, w_up, w_down)
+    )(expert_ids.T, gate_weight.T, expert_map, tokens, w_gate, w_up, w_down)
 
 
 def solution(mesh):

time: 74.4 us -> 58.4 us (0.78)
  Pallas kernels: 69.7 us -> 56.6 us
  local copies, waits for them, and re-layouts: 4.34 us -> 1.64 us
    pallas_call x1, Pallas kernels: 69.7 us -> 56.6 us  [body(): pl.pallas_call(functools.partial(ring_kernel, n), out_shape=jax.ShapeDtyp...]
    unnamed x3 -> x1, local copies, waits for them, and re-layouts: 4.34 us -> 1.64 us
where the time goes in v2:
time: 58.4 us; the launch traced here: 58.3 us
  Pallas kernels  56.6 us (97%)
  local copies, waits for them, and re-layouts  1.64 us (3%)
    pallas_call x1, Pallas kernels, body(): pl.pallas_call(functools.partial(ring_kernel, n), out_shape=jax.ShapeDtyp...  56.6 us
    unnamed x1, local copies, waits for them, and re-layouts  1.64 us

profile of v2, /device:TPU:0, one launch (start us, length us, event | category | flops | bytes accessed | tf_op | source)
XLA Modules:
  0.0 58.3 jit_solution(1820991871632784130)
XLA Ops:
  0.0 56.6 %shard_map.73 = bf16[16,7168]{1,0:T(8,128)(2,1)} custom-call(s32[4,16]{1,0:T(4,128)} %bitcast.2, bf16[4,16]{1,0:T(4,128)(2,1)} %bitcast.3, s32[8]{0:T(128)} %map_ref.1, bf16[16,7168]{1,0:T(8,128)(2,1)} %tokens_ref.1, bf16[1,7168,512]{2,1,0:T(8,128)(2,1)} %wg_hbm.1, bf16[1,7168,512]{2,1,0:T(8,128)(2,1)} %wu_hbm.1, bf16[1,512,7168]{2,1,0:T(8,128)(2,1)} %wd_hbm.1), custom_call_target="tpu_custom_call" | custom-call | flops 5637144576 | bytes 22020096 | tf_op jit(solution)/shard_map/pallas_call | solution.py:218
  56.6 1.6 %copy.9 = bf16[16,7168]{1,0:T(8,128)(2,1)} copy(bf16[16,7168]{1,0:T(8,128)(2,1)} %shard_map.73) | data formatting | bytes 458752

commit v3 on v2

--- a/solution.py
+++ b/solution.py
@@ -180,20 +180,19 @@
         for h in range(pieces):
             gather(s, h)
 
-    def between(gather_step, reduce_step):
+    def between(gather_step, reduce_step, lag):
         def run(h):
+            if 0 < reduce_step < n and h >= lag:
+                reduce(reduce_step, h - lag)
             if gather_step < n:
                 gather(gather_step, h)
-            if 0 < reduce_step < n:
-                reduce(reduce_step, h)
         return run
 
     groups = n // GROUP
     for g in range(groups):
-        hidden = hidden_of(g, between(2 * g + 3, 2 * g - 1))
-        down(g, hidden, between(2 * g + 4, 2 * g))
-    for h in range(pieces):
-        reduce(n - 1, h)
+        hidden = hidden_of(g, between(2 * g + 3, 2 * g, 0))
+        down(g, hidden, between(2 * g + 4, 2 * g + 1, 1))
+        reduce(2 * g + 1, pieces - 1)
     for h in range(pieces):
         out_ref[:, y_cols[h][0]:y_cols[h][0] + y_cols[h][1]] = total(0, h).astype(out_ref.dtype)
 

time: 58.4 us -> 58.9 us (level)
  no operation moved by 1% of the time
where the time goes in v3:
time: 58.9 us; the launch traced here: 58.7 us
  Pallas kernels  57.1 us (97%)
  local copies, waits for them, and re-layouts  1.64 us (3%)
    pallas_call x1, Pallas kernels, body(): pl.pallas_call(functools.partial(ring_kernel, n), out_shape=jax.ShapeDtyp...  57.1 us
    unnamed x1, local copies, waits for them, and re-layouts  1.64 us

profile of v3, /device:TPU:0, one launch (start us, length us, event | category | flops | bytes accessed | tf_op | source)
XLA Modules:
  0.0 58.7 jit_solution(10235944546254545208)
XLA Ops:
  0.0 57.1 %shard_map.73 = bf16[16,7168]{1,0:T(8,128)(2,1)} custom-call(s32[4,16]{1,0:T(4,128)} %bitcast.2, bf16[4,16]{1,0:T(4,128)(2,1)} %bitcast.3, s32[8]{0:T(128)} %map_ref.1, bf16[16,7168]{1,0:T(8,128)(2,1)} %tokens_ref.1, bf16[1,7168,512]{2,1,0:T(8,128)(2,1)} %wg_hbm.1, bf16[1,7168,512]{2,1,0:T(8,128)(2,1)} %wu_hbm.1, bf16[1,512,7168]{2,1,0:T(8,128)(2,1)} %wd_hbm.1), custom_call_target="tpu_custom_call" | custom-call | flops 5637144576 | bytes 22020096 | tf_op jit(solution)/shard_map/pallas_call | solution.py:217
  57.1 1.6 %copy.9 = bf16[16,7168]{1,0:T(8,128)(2,1)} copy(bf16[16,7168]{1,0:T(8,128)(2,1)} %shard_map.73) | data formatting | bytes 458752
